TPU v7x, 512 devices: a whole 4x8x8 slice. The times are simulated.
512 devices in a mesh: rep: 8 (over z), gx: 4 (over y_hi), gy: 4 (over y_lo, core), gz: 4 (over x).
Axes of the slice: x: 4, y: 8 (y_hi: 4, y_lo: 2; y = y_hi * 2 + y_lo), z: 8, core: 2. Of those that a mesh axis runs over, the one named last changes fastest.
Arguments:
- context: bfloat16 [16384, 6144], P(('rep', 'gx'), ('gy', 'gz')), may hold values from -6 to 6
- out_grad: bfloat16 [16384, 6144], P(('rep', 'gy', 'gz'), 'gx'), may hold values from -6 to 6
- kept_values: bfloat16 [3072, 6144], P(('gy', 'gz'), 'gx'), may hold values from -0.109375 to 0.109375
- keep_codes: int32 [1536, 6144], P(('gy', 'gz'), 'gx'), may hold values from 0 to 5
Outputs:
- context_grad: bfloat16 [16384, 6144], P(('rep', 'gx'), ('gy', 'gz'))
- kept_grad: bfloat16 [3072, 6144], P(('gy', 'gz'), 'gx')
Inputs may be any that keep to these rules, and one draw needn't show every extreme that they name: `keep_codes`: code 0 keeps positions (0, 1), 1 keeps (0, 2), 2 keeps (0, 3), 3 keeps (1, 2), 4 keeps (1, 3), 5 keeps (2, 3) of its group of four input rows.
All inputs are finite; a program needn't handle non-finite values.
Results may differ from a plain program's by a relative error of at most 0.001.
Values may be sent and summed in bfloat16 or wider, within the bound.
A program may use at most 64 MiB of HBM per device.

v0:
```python
import jax
import jax.numpy as jnp
from jax import lax
from jax.sharding import PartitionSpec as P


def kept_positions(codes):
    lower_pos = jnp.where(codes < 3, 0, jnp.where(codes < 5, 1, 2)).astype(jnp.int32)
    upper_pos = jnp.where(codes == 0, 1, jnp.where((codes == 1) | (codes == 3), 2, 3)).astype(
        jnp.int32
    )
    return (lower_pos, upper_pos)


def expand_pairs(values, codes):
    groups, columns = codes.shape
    lower_pos, upper_pos = kept_positions(codes)
    paired = values.reshape(groups, 2, columns)
    slot_ids = jnp.arange(4, dtype=jnp.int32)[None, :, None]
    zero_value = jnp.zeros((), values.dtype)
    dense = jnp.where(
        slot_ids == lower_pos[:, None, :],
        paired[:, 0:1, :],
        jnp.where(slot_ids == upper_pos[:, None, :], paired[:, 1:2, :], zero_value),
    )
    return dense.reshape(4 * groups, columns)


def compress_pairs(dense, codes):
    groups, columns = codes.shape
    lower_pos, upper_pos = kept_positions(codes)
    blocks = dense.reshape(groups, 4, columns)
    slot_ids = jnp.arange(4, dtype=jnp.int32)[None, :, None]
    zero_value = jnp.zeros((), dense.dtype)
    first_kept = jnp.sum(jnp.where(slot_ids == lower_pos[:, None, :], blocks, zero_value), axis=1)
    second_kept = jnp.sum(jnp.where(slot_ids == upper_pos[:, None, :], blocks, zero_value), axis=1)
    return jnp.stack([first_kept, second_kept], axis=1).reshape(2 * groups, columns)


def times_weight(grad_rows, dense_w):
    return lax.dot_general(
        grad_rows, dense_w, (((1,), (1,)), ((), ())), preferred_element_type=jnp.float32
    )


def over_tokens(context_rows, grad_rows):
    return lax.dot_general(
        context_rows, grad_rows, (((0,), (0,)), ((), ())), preferred_element_type=jnp.float32
    )


def local(context, out_grad, kept_values, keep_codes):
    dense_w = expand_pairs(kept_values, keep_codes)
    rows_all = lax.all_gather(context, "gx", axis=0, tiled=True)
    grad_scale = (lax.axis_size("rep") * rows_all.shape[0]) ** (-0.5)
    grads_all = lax.all_gather(out_grad, ("gy", "gz"), axis=0, tiled=True)
    partial_in = times_weight(grads_all, dense_w)
    weight_part = over_tokens(rows_all, grads_all)
    context_grad = lax.psum_scatter(partial_in, "gx", scatter_dimension=0, tiled=True)
    kept_sum = lax.psum(compress_pairs(weight_part, keep_codes), "rep") * grad_scale
    return (context_grad.astype(jnp.bfloat16), kept_sum.astype(jnp.bfloat16))


def solution(mesh):
    in_specs = (
        P(("rep", "gx"), ("gy", "gz")),
        P(("rep", "gy", "gz"), "gx"),
        P(("gy", "gz"), "gx"),
        P(("gy", "gz"), "gx"),
    )
    out_specs = (P(("rep", "gx"), ("gy", "gz")), P(("gy", "gz"), "gx"))
    return jax.shard_map(local, mesh=mesh, in_specs=in_specs, out_specs=out_specs, check_vma=False)
```

profile of v0, /device:TPU:1, one launch (start us, length us, event | category | flops | bytes accessed | tf_op | source)
XLA Modules:
  0.0 300.9 jit_solution(17981077440742864799)
XLA Ops:
  7.2 0.0 copy-start.4
  7.2 0.0 all-gather.5.cloned.1.call-start
  7.2 0.7 all-gather.5.cloned.1.call-update
  7.9 0.0 all-gather.3.cloned.1.call-start
  8.0 0.7 all-gather.3.cloned.1.call-update
  8.7 0.0 all-reduce.2.cloned.1.call-start
  8.7 0.1 eq.75
  8.8 1.9 reshape.22
  10.7 1.8 fusion.3
  12.6 0.0 copy-done.4
  12.6 0.2 select_select_fusion
  12.8 48.5 %all-gather.5.cloned.1.call-done = bf16[2048,384]{1,0:T(8,128)(2,1)} async-done(((bf16[512,384]{1,0:T(8,128)(2,1)}), bf16[2048,384]{1,0:T(8,128)(2,1)}) %all-gather.5.cloned.1.call-update) | async-done | bytes 1572880 | tf_op jit(solution)/shard_map/all_gather | solution.py:54
  61.3 58.9 %all-gather.3.cloned.1.call-done = bf16[2048,1536]{1,0:T(8,128)(2,1)} async-done(((bf16[128,1536]{1,0:T(8,128)(2,1)}), bf16[2048,1536]{1,0:T(8,128)(2,1)}) %all-gather.3.cloned.1.call-update) | async-done | bytes 6291472 | tf_op jit(solution)/shard_map/all_gather | solution.py:56
  120.1 7.4 %fusion.4 = f32[384,1536]{1,0:T(8,128)} fusion(bf16[2048,384]{1,0:T(8,128)(2,1)} %all-gather.5.cloned.1.call-done, bf16[2048,1536]{1,0:T(8,128)(2,1)} %all-gather.3.cloned.1.call-done), kind=kOutput, calls=%fused_computation.17 | convolution fusion | flops 2415919104 | bytes 10223616 | tf_op jit(solution)/shard_map/dot_general | solution.py:47
  127.5 2.6 reshape.23
  130.1 3.6 %select_reduce_fusion.1 = (f32[96,1536]{1,0:T(8,128)S(1)}, f32[96,1536]{1,0:T(8,128)S(1)}) fusion(f32[96,4,1536]{2,1,0:T(4,128)S(1)} %reshape.23, s32[96,1536]{1,0:T(8,128)S(1)} %get-tuple-element.11, s32[96,1536]{1,0:T(8,128)S(1)} %get-tuple-element.10), kind=kLoop, calls=%fused_computation.3 | loop fusion | flops 3244032 | bytes 4718592 | tf_op jit(solution)/shard_map/reduce_sum | solution.py:35
  133.7 0.4 stack.9
  134.1 0.4 stack.10
  134.6 1.1 pad_maximum_fusion
  135.6 0.0 copy-start.1
  135.6 0.0 copy-start.2
  135.6 1.9 reshape.24
  137.5 0.0 all-reduce.2.cloned.1.call-update
  137.5 0.2 reduce-scatter.2.cloned.1.call-start
  137.8 0.0 copy-done.1
  137.8 0.0 copy-done.2
  137.8 0.8 copy_bitcast_fusion
  138.6 0.0 copy-start.3
  138.6 0.3 broadcast_in_dim.67
  138.9 1.2 broadcast_in_dim.68
  140.1 0.0 copy-done.3
  140.1 0.3 broadcast_in_dim.64
  140.4 1.2 broadcast_in_dim.65
  141.6 0.4 eq.83
  142.0 1.9 eq.84
  143.9 0.4 eq.77
  144.3 0.0 copy-start
  144.3 1.9 eq.78
  146.2 0.0 copy-done
  146.2 9.0 %convolution_bitcast_fusion = f32[2048,384]{0,1:T(8,128)} fusion(bf16[2048,1536]{1,0:T(8,128)(2,1)} %all-gather.3.cloned.1.call-done, bf16[384,1536]{1,0:T(8,128)(2,1)} %broadcast_in_dim.65, s32[384,1536]{1,0:T(8,128)} %eq.78, bf16[384,1536]{1,0:T(8,128)(2,1)S(1)} %copy-done, s32[384,1536]{1,0:T(8,128)} %eq.84, s32[384]{0:T(512)S(1)} %eq.75), kind=kOutput, calls=%fused_computation | convolution fusion | flops 2418278400 | bytes 16516608 | tf_op jit(solution)/shard_map/dot_general | solution.py:41
  155.2 0.0 reduce-scatter.2.cloned.1.call-update
  155.2 62.5 %all-reduce.2.cloned.1.call-done = f32[192,1536]{1,0:T(8,128)} async-done(((f32[192,1536]{1,0:T(8,128)}), f32[192,1536]{1,0:T(8,128)}) %all-reduce.2.cloned.1.call-update) | async-done | bytes 1179664 | tf_op jit(solution)/shard_map/psum | solution.py:60
  217.7 2.2 multiply_convert_fusion
  219.8 72.5 %reduce-scatter.2.cloned.1.call-done = f32[512,384]{0,1:T(8,128)} async-done(((f32[2048,384]{0,1:T(8,128)}), f32[512,384]{0,1:T(8,128)}) %reduce-scatter.2.cloned.1.call-update) | async-done | bytes 786448 | tf_op jit(solution)/shard_map/reduce_scatter | solution.py:59
  292.3 1.2 convert_element_type.6
  293.4 0.9 copy.8
  (1 shorter events, 0.0 us)
Async XLA Ops:
  7.2 5.4 %copy-start.4 = (s32[96,1536]{1,0:T(8,128)S(1)}, s32[96,1536]{1,0:T(8,128)}, u32[]{:S(2)}) copy-start(s32[96,1536]{1,0:T(8,128)} %param.7) | copy-start | bytes 1769476
  7.2 54.1 %all-gather.5.cloned.1.call-start = ((), (), s32[]{:S(2)}) async-start(), calls=%async_computation.3 | async-start | bytes 1966080 | tf_op jit(solution)/shard_map/all_gather | solution.py:54
  7.9 112.2 %all-gather.3.cloned.1.call-start = ((), (), s32[]{:S(2)}) async-start(), calls=%async_computation.1 | async-start | bytes 6684672 | tf_op jit(solution)/shard_map/all_gather | solution.py:56
  8.7 209.0 %all-reduce.2.cloned.1.call-start = ((), (), s32[]{:S(2)}) async-start(), calls=%async_computation.4 | async-start | bytes 2359296 | tf_op jit(solution)/shard_map/psum | solution.py:60
  135.6 2.1 copy-start.1
  135.6 2.1 copy-start.2
  137.5 154.7 %reduce-scatter.2.cloned.1.call-start = ((), (), s32[]{:S(2)}) async-start(), calls=%async_computation.2 | async-start | bytes 3932160 | tf_op jit(solution)/shard_map/reduce_scatter | solution.py:59
  138.6 1.5 copy-start.3
  144.3 1.9 copy-start
Sparse Core Ops, SparseCore 0:
  10.1 51.1 all-gather.4
  63.4 56.7 all-gather.2
  137.7 79.9 all-reduce.1
  220.4 71.8 reduce-scatter.1
where the time goes:
time: 301 us
  waiting for transfers between devices  244 us (81%)
  local copies, waits for them, and re-layouts  18.4 us (6%)
  matrix products  16.3 us (5%)
  between operations  13.9 us (5%)
  other arithmetic  8.21 us (3%)
    reduce_scatter x1, waiting for transfers between devices, local(): lax.psum_scatter(partial_in, 'gx', scatter_dimension=0, tiled=True)  72.5 us
    psum x1, waiting for transfers between devices, local(): lax.psum(compress_pairs(weight_part, keep_codes), 'rep') * grad_scale  62.5 us
    all_gather x1, waiting for transfers between devices, local(): grads_all = lax.all_gather(out_grad, ('gy', 'gz'), axis=0, tiled=True)  58.9 us
    all_gather x1, waiting for transfers between devices, local(): rows_all = lax.all_gather(context, 'gx', axis=0, tiled=True)  48.5 us
    dot_general x1, matrix products, times_weight(): lax.dot_general(grad_rows, dense_w, (((1,), (1,)), ((), ())), preferred_e...  8.98 us
    dot_general x1, matrix products, over_tokens(): lax.dot_general(context_rows, grad_rows, (((0,), (0,)), ((), ())), prefer...  7.37 us
  transfers between devices with their start and end apart: 4, of which 4 were waited for; matrix products, arithmetic and copies ran while one was open for 8% of the time, Pallas kernels for 0%

commit v1 on v0

v1 whole, which is shorter than its diff:
```python
import jax
import jax.numpy as jnp
from jax import lax
from jax.experimental import pallas as pl
from jax.experimental.pallas import tpu as pltpu
from jax.sharding import PartitionSpec as P

MESH = pl.DeviceIdType.MESH
BF = jnp.bfloat16
F32 = jnp.float32

def dot_nn(a, b):
    return lax.dot_general(a, b, (((1,), (0,)), ((), ())), preferred_element_type=F32)

def dot_nt(a, b):
    return lax.dot_general(a, b, (((1,), (1,)), ((), ())), preferred_element_type=F32)

def one_hot(rows, cols, hit):
    r = lax.broadcasted_iota(jnp.int32, (rows, cols), 0)
    c = lax.broadcasted_iota(jnp.int32, (rows, cols), 1)
    return jnp.where(hit(r, c), 1.0, 0.0).astype(BF)

def kernel(
    ctx_hbm, grad_hbm, kept_hbm, codes_hbm, cg_ref, kg_ref,
    gb, cb, cpt, ws, kept_v, codes_v, rs_out, rs_in, ag, acc,
    load_sem, gs, gr, ts, tr, cs, cr, wys, wyr, wzs, wzr, rss, rsr, ags, agr,
):
    z = lax.axis_index("rep")
    q = lax.axis_index("gx")
    p = lax.axis_index("gy")
    x = lax.axis_index("gz")
    core = p % 2
    twin_p = (p + 2) % 4
    core_p = p + 1 - 2 * core
    core_twin_p = (core_p + 2) % 4
    xr, xl = (x + 1) % 4, (x + 3) % 4
    qr, ql, qo = (q + 1) % 4, (q + 3) % 4, (q + 2) % 4
    up = 1 - 2 * core

    at_twin = (z, q, twin_p, x)
    at_core = (z, q, core_p, x)
    at_xr = (z, q, p, xr)
    at_xl = (z, q, p, xl)
    at_qr = (z, qr, p, x)
    at_ql = (z, ql, p, x)
    at_flip = (z, p, q, x)

    def at_z(step):
        return ((z + step + 8) % 8, q, p, x)

    sends = []

    def copy(src, dst, ssem, rsem, device):
        return pltpu.make_async_remote_copy(
            src_ref=src, dst_ref=dst, send_sem=ssem, recv_sem=rsem,
            device_id=device, device_id_type=MESH,
        )

    loads = []
    for k in range(4):
        loads.append(pltpu.make_async_copy(
            grad_hbm.at[:, pl.ds(k * 384, 384)], gb.at[0, k, p, x], load_sem.at[k]))
    for j in range(3):
        loads.append(pltpu.make_async_copy(
            ctx_hbm.at[:, pl.ds(j * 128, 128)], cb.at[q, j], load_sem.at[4 + j]))
    loads.append(pltpu.make_async_copy(kept_hbm, kept_v, load_sem.at[7]))
    loads.append(pltpu.make_async_copy(codes_hbm, codes_v, load_sem.at[8]))
    for ld in loads:
        ld.start()

    barrier = pltpu.get_barrier_semaphore()
    for device in [at_twin, at_core, at_xr, at_xl, at_qr, at_ql] + [at_z(s) for s in range(1, 8)]:
        pl.semaphore_signal(barrier, inc=1, device_id=device, device_id_type=MESH)

    @pl.when(p != q)
    def _():
        pl.semaphore_signal(barrier, inc=1, device_id=at_flip, device_id_type=MESH)

    for ld in loads:
        ld.wait()
    split = one_hot(192, 192, lambda r, c: c == 2 * (r % 96) + r // 96)
    for k in range(4):
        cols = pl.ds(k * 384, 384)
        both = dot_nn(split, kept_v[:, cols]).astype(BF)
        numbers = codes_v[:, cols].astype(F32).astype(BF)
        ws[q, k] = both[:144]
        ws[q, 4 + k, 0:48] = both[144:]
        ws[q, 4 + k, 48:144] = numbers

    pl.semaphore_wait(barrier, jnp.where(p != q, 14, 13))

    def guarded(ph, block_p, run):
        if ph == 0:
            run()
        else:
            pl.when(block_p != q)(run)

    def g_copy(ph, k, block, si, ri, device):
        ref = gb.at[ph, k, block[0], block[1]]
        return copy(ref, ref, gs.at[ph * 4 + k, si], gr.at[ph * 4 + k, ri], device)

    def g_send(ph, k, block, si, ri, device):
        guarded(ph, block[0], lambda: g_copy(ph, k, block, si, ri, device).start())
        sends.append(lambda: guarded(
            ph, block[0], lambda: g_copy(ph, k, block, si, ri, device).wait_send()))

    def g_wait(ph, k, block, ri):
        guarded(ph, block[0], lambda: g_copy(ph, k, block, 0, ri, at_core).wait_recv())

    def g_row(ph, k, block_p, si, ri):
        ref = gb.at[ph, k, block_p]
        return copy(ref, ref, gs.at[ph * 4 + k, si], gr.at[ph * 4 + k, ri], at_core)

    def g_core(ph, k, block_p, si, ri):
        guarded(ph, block_p, lambda: g_row(ph, k, block_p, si, ri).start())
        sends.append(lambda: guarded(
            ph, block_p, lambda: g_row(ph, k, block_p, si, ri).wait_send()))

    def g_core_wait(ph, k):
        guarded(ph, core_p, lambda: g_row(ph, k, core_p, 7, 7).wait_recv())
        guarded(ph, core_twin_p, lambda: g_row(ph, k, core_twin_p, 8, 8).wait_recv())

    def g_twin_send(ph, k):
        g_send(ph, k, (p, x), 0, 0, at_twin)

    def g_own(ph, k):
        g_send(ph, k, (p, x), 1, 1, at_xr)
        g_send(ph, k, (p, x), 2, 2, at_xl)

    def g_twin(ph, k):
        g_wait(ph, k, (twin_p, x), 0)
        g_send(ph, k, (twin_p, x), 3, 3, at_xr)
        g_send(ph, k, (twin_p, x), 4, 4, at_xl)

    def g_forward(ph, k):
        g_wait(ph, k, (p, xl), 1)
        g_send(ph, k, (p, xl), 5, 5, at_xr)
        g_wait(ph, k, (twin_p, xr), 4)
        g_send(ph, k, (twin_p, xr), 6, 6, at_xl)

    def g_last(ph, k):
        g_wait(ph, k, (p, xr), 2)
        g_wait(ph, k, (twin_p, xl), 3)
        g_wait(ph, k, (p, (x + 2) % 4), 5)
        g_core(ph, k, p, 7, 7)
        g_wait(ph, k, (twin_p, (x + 2) % 4), 6)
        g_core(ph, k, twin_p, 8, 8)

    def t_copy(k):
        return copy(gb.at[0, k, p, x], gb.at[1, k, q, x], ts.at[k], tr.at[k], at_flip)

    def t_send(k):
        pl.when(p != q)(lambda: t_copy(k).start())
        sends.append(lambda: pl.when(p != q)(lambda: t_copy(k).wait_send()))

    def t_wait(k):
        pl.when(p != q)(lambda: copy(
            gb.at[1, k, p, x], gb.at[1, k, p, x], ts.at[k], tr.at[k], at_flip).wait_recv())

    def c_copy(j, block_q, ri, device):
        if ri < 2:
            ref = cb.at[block_q, j]
        else:
            ref = cb.at[block_q, j, pl.ds((ri - 2) * 256, 256)]
        return copy(ref, ref, cs.at[j, ri], cr.at[j, ri], device)

    def c_send(j, block_q, ri, device):
        c_copy(j, block_q, ri, device).start()
        sends.append(lambda: c_copy(j, block_q, ri, device).wait_send())

    def c_own(j):
        c_send(j, q, 0, at_qr)
        c_send(j, q, 1, at_ql)

    def c_forward(j):
        c_copy(j, ql, 0, at_qr).wait_recv()
        c_send(j, ql, 2, at_qr)
        c_copy(j, qr, 1, at_qr).wait_recv()
        c_send(j, qr, 3, at_ql)

    def c_last(j):
        c_copy(j, qo, 2, at_qr).wait_recv()
        c_copy(j, qo, 3, at_qr).wait_recv()

    def wy_copy(block_q, ri, device):
        ref = ws.at[block_q, z]
        return copy(ref, ref, wys.at[ri], wyr.at[ri], device)

    def wy_own():
        for ri, device in ((0, at_qr), (1, at_ql)):
            wy_copy(q, ri, device).start()
            sends.append(lambda ri=ri, device=device: wy_copy(q, ri, device).wait_send())

    def wy_forward():
        wy_copy(ql, 0, at_qr).wait_recv()
        pl.when(core == 0)(lambda: wy_copy(ql, 2, at_qr).start())
        wy_copy(qr, 1, at_qr).wait_recv()
        pl.when(core == 1)(lambda: wy_copy(qr, 2, at_ql).start())
        sends.append(lambda: wy_copy(ql, 2, at_qr).wait_send())

    def wz_copy(m, block_q, slice_z, ri, device):
        ref = ws.at[block_q, slice_z]
        return copy(ref, ref, wzs.at[m, ri], wzr.at[m, ri], device)

    def wz_send(m, step):
        block_q = (ql, qr, qo)[m]
        todo = []
        if step <= 4:
            todo.append(((z - (step - 1) * up + 8) % 8, step - 1, at_z(up)))
        if step <= 3:
            todo.append(((z + (step - 1) * up + 8) % 8, 3 + step, at_z(-up)))
        for slice_z, ri, device in todo:
            wz_copy(m, block_q, slice_z, ri, device).start()
            sends.append(lambda a=(m, block_q, slice_z, ri, device): wz_copy(*a).wait_send())

    def wz_wait(m, step):
        block_q = (ql, qr, qo)[m]
        wz_copy(m, block_q, (z - step * up + 8) % 8, step - 1, at_core).wait_recv()
        if step <= 3:
            wz_copy(m, block_q, (z + step * up + 8) % 8, 3 + step, at_core).wait_recv()

    def kg_part(j):
        turn = one_hot(128, 128, lambda r, c: c == 4 * (r % 32) + r // 32)
        for b in range(4):
            cpt[:, b * 512:(b + 1) * 512] = dot_nt(turn, cb[b, j]).astype(BF)

        for k in range(4):
            cols = pl.ds(k * 384, 384)
            dense = dot_nn(cpt[...], gb[0, k].reshape(2048, 384))
            codes = codes_v[32 * j:32 * j + 32, cols]
            d0, d1, d2, d3 = (dense[32 * s:32 * s + 32] for s in range(4))
            first = jnp.where(codes < 3, d0, jnp.where(codes < 5, d1, d2))
            second = jnp.where(
                codes == 0, d1, jnp.where((codes == 1) | (codes == 3), d2, d3))
            for s in range(4):
                rs_out[j, s, :, cols] = first[8 * s:8 * s + 8]
                rs_out[j, 4 + s, :, cols] = second[8 * s:8 * s + 8]

    def rs_copy(j, step):
        return copy(rs_out.at[j, (z + step) % 8], rs_in.at[j, step - 1],
                    rss.at[j, step - 1], rsr.at[j, step - 1], at_z(step))

    def rs_send(j):
        for step in (4, 3, 5, 2, 6, 1, 7):
            rs_copy(j, step).start()
            sends.append(lambda step=step: rs_copy(j, step).wait_send())

    def ag_copy(j, step, slice_z):
        ref = ag.at[j, slice_z]
        return copy(ref, ref, ags.at[j, step - 1], agr.at[j, step - 1], at_z(step))

    def rs_finish(j):
        for step in range(1, 8):
            rs_copy(j, step).wait_recv()
        total = rs_out[j, z]
        for step in range(7):
            total = total + rs_in[j, step]
        total = total * (16384.0 ** -0.5)
        ag[j, z] = jnp.concatenate([total[:, :768], total[:, 768:]], 0).astype(BF)
        for step in (4, 3, 5, 2, 6, 1, 7):
            ag_copy(j, step, z).start()
            sends.append(lambda step=step: ag_copy(j, step, z).wait_send())

    def ag_wait(j):
        for step in range(1, 8):
            ag_copy(j, step, (z - step + 8) % 8).wait_recv()

    def kg_store():
        rows = ag[...].reshape(384, 768)
        for h in range(2):
            def hit(r, c, h=h):
                slot, group = r % 2, r // 2
                want = (((group // 32) * 8 + slot * 4 + (group % 32) // 8) * 2 + h) * 8 + group % 8
                return c == want

            kg_ref[:, h * 768:(h + 1) * 768] = dot_nn(one_hot(192, 384, hit), rows).astype(BF)

    def weights(block_q, k):
        top, low = ws[block_q, k], ws[block_q, 4 + k]
        k0 = top[:96].astype(F32)
        k1 = jnp.concatenate([top[96:], low[:48]], 0).astype(F32)
        code = low[48:].astype(F32)
        w0 = jnp.where(code < 2.5, k0, 0.0)
        w1 = jnp.where(code < 0.5, k1, jnp.where((code > 2.5) & (code < 4.5), k0, 0.0))
        is2 = ((code > 0.5) & (code < 1.5)) | ((code > 2.5) & (code < 3.5))
        w2 = jnp.where(code > 4.5, k0, jnp.where(is2, k1, 0.0))
        is3 = ((code > 1.5) & (code < 2.5)) | (code > 3.5)
        w3 = jnp.where(is3, k1, 0.0)
        return jnp.concatenate([w0, w1, w2, w3], 0).astype(BF)

    def cg_own():
        total = jnp.zeros((512, 384), F32)
        for k in range(4):
            total = total + dot_nt(gb[0, k, q].reshape(512, 384), weights(q, k))
        acc[...] = total

    def cg_add(k):
        for b in (ql, qr, qo):
            acc[...] += dot_nt(gb[1, k, b].reshape(512, 384), weights(b, k))

    def cg_store():
        back = one_hot(384, 384, lambda r, c: c == 4 * (r % 96) + r // 96)
        cg_ref[...] = dot_nn(acc[...].astype(BF), back).astype(BF)

    for k in range(4):
        g_twin_send(0, k)
        g_own(0, k)
    wy_own()
    c_own(0)
    g_twin(0, 0)
    wy_forward()
    wz_send(0, 1)
    wz_send(1, 1)
    g_forward(0, 0)
    c_own(1)
    g_twin(0, 1)
    wy_copy(qo, 2, at_qr).wait_recv()
    wz_send(2, 1)
    c_forward(0)
    g_forward(0, 1)
    g_last(0, 0)
    c_own(2)
    g_twin(0, 2)
    for m in range(3):
        wz_wait(m, 1)
        wz_send(m, 2)
    g_forward(0, 2)
    g_last(0, 1)
    for k in range(4):
        t_send(k)
    g_twin(0, 3)
    c_last(0)
    c_forward(1)
    for m in range(3):
        wz_wait(m, 2)
        wz_send(m, 3)
    g_forward(0, 3)
    g_last(0, 2)
    c_forward(2)
    g_last(0, 3)
    for m in range(3):
        wz_wait(m, 3)
        wz_send(m, 4)
    for k in range(4):
        g_core_wait(0, k)
    c_last(1)
    for k in range(4):
        t_wait(k)
        g_twin_send(1, k)
        g_own(1, k)
    kg_part(0)
    rs_send(0)
    g_twin(1, 0)
    g_forward(1, 0)
    kg_part(1)
    rs_send(1)
    g_twin(1, 1)
    g_forward(1, 1)
    g_last(1, 0)
    c_last(2)
    kg_part(2)
    rs_send(2)
    g_twin(1, 2)
    g_forward(1, 2)
    g_last(1, 1)
    rs_finish(0)
    cg_own()
    g_twin(1, 3)
    g_forward(1, 3)
    g_last(1, 2)
    for m in range(3):
        wz_wait(m, 4)
    rs_finish(1)
    g_core_wait(1, 0)
    cg_add(0)
    g_last(1, 3)
    g_core_wait(1, 1)
    cg_add(1)
    rs_finish(2)
    g_core_wait(1, 2)
    cg_add(2)
    g_core_wait(1, 3)
    cg_add(3)
    cg_store()
    for j in range(3):
        ag_wait(j)
    kg_store()
    for wait in sends:
        wait()

def local(context, out_grad, kept_values, keep_codes):
    dma = pltpu.SemaphoreType.DMA
    return pl.pallas_call(
        kernel,
        out_shape=(
            jax.ShapeDtypeStruct((512, 384), BF),
            jax.ShapeDtypeStruct((192, 1536), BF),
        ),
        in_specs=[pl.BlockSpec(memory_space=pl.ANY)] * 4,
        out_specs=(pl.BlockSpec(memory_space=pltpu.VMEM),) * 2,
        scratch_shapes=[
            pltpu.VMEM((2, 4, 4, 4, 128, 384), BF),
            pltpu.VMEM((4, 3, 512, 128), BF),
            pltpu.VMEM((128, 2048), BF),
            pltpu.VMEM((4, 8, 144, 384), BF),
            pltpu.VMEM((192, 1536), BF),
            pltpu.VMEM((96, 1536), jnp.int32),
            pltpu.VMEM((3, 8, 8, 1536), F32),
            pltpu.VMEM((3, 7, 8, 1536), F32),
            pltpu.VMEM((3, 8, 16, 768), BF),
            pltpu.VMEM((512, 384), F32),
            dma((9,)),

            dma((8, 9)),
            dma((8, 9)),
            dma((4,)),
            dma((4,)),
            dma((3, 4)),
            dma((3, 4)),
            dma((3,)),
            dma((3,)),
            dma((3, 7)),
            dma((3, 7)),
            dma((3, 7)),
            dma((3, 7)),
            dma((3, 7)),
            dma((3, 7)),
        ],
        compiler_params=pltpu.CompilerParams(
            collective_id=0, has_side_effects=True, vmem_limit_bytes=56 << 20
        ),
        cost_estimate=pl.CostEstimate(
            flops=4 * 2048 * 384 * 1536, bytes_accessed=3 << 20, transcendentals=0
        ),
        name="sparse_backward",
    )(context, out_grad, kept_values, keep_codes)

def solution(mesh):
    in_specs = (
        P(("rep", "gx"), ("gy", "gz")),
        P(("rep", "gy", "gz"), "gx"),
        P(("gy", "gz"), "gx"),
        P(("gy", "gz"), "gx"),
    )
    out_specs = (P(("rep", "gx"), ("gy", "gz")), P(("gy", "gz"), "gx"))
    return jax.shard_map(local, mesh=mesh, in_specs=in_specs, out_specs=out_specs, check_vma=False)
```

time: 301 us -> 117 us (0.39)
  the two profiles are of different devices: /device:TPU:1 before, /device:TPU:21 now
where the time goes in v1:
time: 117 us
  Pallas kernels  113 us (97%)
  local copies, waits for them, and re-layouts  2.66 us (2%)
    pallas_call x1, Pallas kernels, local(): pl.pallas_call(kernel, out_shape=(jax.ShapeDtypeStruct((512, 384), BF), j...  113 us
    unnamed x4, local copies, waits for them, and re-layouts  2.66 us

profile of v1, /device:TPU:21, one launch (start us, length us, event | category | flops | bytes accessed | tf_op | source)
XLA Modules:
  0.0 116.7 jit_solution(16417725546010397340)
XLA Ops:
  0.6 113.4 %sparse_backward.1 = (bf16[512,384]{1,0:T(8,128)(2,1)}, bf16[192,1536]{1,0:T(8,128)(2,1)}) custom-call(bf16[512,384]{1,0:T(8,128)(2,1)} %ctx_hbm.1, bf16[128,1536]{1,0:T(8,128)(2,1)} %grad_hbm.1, bf16[192,1536]{1,0:T(8,128)(2,1)} %kept_hbm.1, s32[96,1536]{1,0:T(8,128)} %codes_hbm.1), custom_call_target="tpu_custom_call" | custom-call | flops 4831838208 | bytes 3145728 | tf_op jit(solution)/shard_map/sparse_backward/pallas_call | solution.py:393
  114.0 0.0 copy-start
  114.0 1.8 %copy.8 = bf16[512,384]{1,0:T(8,128)(2,1)} copy(bf16[512,384]{1,0:T(8,128)(2,1)} %get-tuple-element.4) | data formatting | bytes 786432
  115.9 0.0 copy-done
  115.9 0.8 copy.9
Async XLA Ops:
  114.0 1.9 %copy-start = (bf16[192,1536]{1,0:T(8,128)(2,1)S(1)}, bf16[192,1536]{1,0:T(8,128)(2,1)}, u32[]{:S(2)}) copy-start(bf16[192,1536]{1,0:T(8,128)(2,1)} %get-tuple-element.5) | copy-start | bytes 1769476

commit v2 on v1

--- a/solution.py
+++ b/solution.py
@@ -43,7 +43,9 @@
     at_xl = (z, q, p, xl)
     at_qr = (z, qr, p, x)
     at_ql = (z, ql, p, x)
-    at_flip = (z, p, q, x)
+    delta = (p - q + 4) % 4
+    t_slots = ((delta * delta - delta) // 2, (delta // 2) * delta)
+    at_source = (z, (q + 3 - (p + 1) // 2) % 4, q, x)
 
     def at_z(step):
         return ((z + step + 8) % 8, q, p, x)
@@ -72,9 +74,17 @@
     for device in [at_twin, at_core, at_xr, at_xl, at_qr, at_ql] + [at_z(s) for s in range(1, 8)]:
         pl.semaphore_signal(barrier, inc=1, device_id=device, device_id_type=MESH)
 
-    @pl.when(p != q)
+    pl.semaphore_signal(barrier, inc=1, device_id=at_source, device_id_type=MESH)
+
+    @pl.when(delta != 0)
     def _():
-        pl.semaphore_signal(barrier, inc=1, device_id=at_flip, device_id_type=MESH)
+        pl.semaphore_signal(
+            barrier, inc=1, device_id=(z, p, t_slots[0], x), device_id_type=MESH)
+
+    @pl.when(delta == 2)
+    def _():
+        pl.semaphore_signal(
+            barrier, inc=1, device_id=(z, p, t_slots[1], x), device_id_type=MESH)
 
     for ld in loads:
         ld.wait()
@@ -87,38 +97,38 @@
         ws[q, 4 + k, 0:48] = both[144:]
         ws[q, 4 + k, 48:144] = numbers
 
-    pl.semaphore_wait(barrier, jnp.where(p != q, 14, 13))
-
-    def guarded(ph, block_p, run):
+    pl.semaphore_wait(barrier, jnp.where(delta == 0, 14, jnp.where(delta == 2, 16, 15)))
+
+    def guarded(ph, k, block_p, run):
         if ph == 0:
             run()
         else:
-            pl.when(block_p != q)(run)
+            pl.when(block_p != (2 if k < 2 else 1))(run)
 
     def g_copy(ph, k, block, si, ri, device):
         ref = gb.at[ph, k, block[0], block[1]]
         return copy(ref, ref, gs.at[ph * 4 + k, si], gr.at[ph * 4 + k, ri], device)
 
     def g_send(ph, k, block, si, ri, device):
-        guarded(ph, block[0], lambda: g_copy(ph, k, block, si, ri, device).start())
+        guarded(ph, k, block[0], lambda: g_copy(ph, k, block, si, ri, device).start())
         sends.append(lambda: guarded(
-            ph, block[0], lambda: g_copy(ph, k, block, si, ri, device).wait_send()))
+            ph, k, block[0], lambda: g_copy(ph, k, block, si, ri, device).wait_send()))
 
     def g_wait(ph, k, block, ri):
-        guarded(ph, block[0], lambda: g_copy(ph, k, block, 0, ri, at_core).wait_recv())
+        guarded(ph, k, block[0], lambda: g_copy(ph, k, block, 0, ri, at_core).wait_recv())
 
     def g_row(ph, k, block_p, si, ri):
         ref = gb.at[ph, k, block_p]
         return copy(ref, ref, gs.at[ph * 4 + k, si], gr.at[ph * 4 + k, ri], at_core)
 
     def g_core(ph, k, block_p, si, ri):
-        guarded(ph, block_p, lambda: g_row(ph, k, block_p, si, ri).start())
+        guarded(ph, k, block_p, lambda: g_row(ph, k, block_p, si, ri).start())
         sends.append(lambda: guarded(
-            ph, block_p, lambda: g_row(ph, k, block_p, si, ri).wait_send()))
+            ph, k, block_p, lambda: g_row(ph, k, block_p, si, ri).wait_send()))
 
     def g_core_wait(ph, k):
-        guarded(ph, core_p, lambda: g_row(ph, k, core_p, 7, 7).wait_recv())
-        guarded(ph, core_twin_p, lambda: g_row(ph, k, core_twin_p, 8, 8).wait_recv())
+        guarded(ph, k, core_p, lambda: g_row(ph, k, core_p, 7, 7).wait_recv())
+        guarded(ph, k, core_twin_p, lambda: g_row(ph, k, core_twin_p, 8, 8).wait_recv())
 
     def g_twin_send(ph, k):
         g_send(ph, k, (p, x), 0, 0, at_twin)
@@ -132,30 +142,35 @@
         g_send(ph, k, (twin_p, x), 3, 3, at_xr)
         g_send(ph, k, (twin_p, x), 4, 4, at_xl)
 
-    def g_forward(ph, k):
+    def g_fwd_own(ph, k):
         g_wait(ph, k, (p, xl), 1)
         g_send(ph, k, (p, xl), 5, 5, at_xr)
+
+    def g_fwd_twin(ph, k):
         g_wait(ph, k, (twin_p, xr), 4)
         g_send(ph, k, (twin_p, xr), 6, 6, at_xl)
 
-    def g_last(ph, k):
+    def g_core_own(ph, k):
         g_wait(ph, k, (p, xr), 2)
-        g_wait(ph, k, (twin_p, xl), 3)
         g_wait(ph, k, (p, (x + 2) % 4), 5)
         g_core(ph, k, p, 7, 7)
+
+    def g_core_twin(ph, k):
+        g_wait(ph, k, (twin_p, xl), 3)
         g_wait(ph, k, (twin_p, (x + 2) % 4), 6)
         g_core(ph, k, twin_p, 8, 8)
 
     def t_copy(k):
-        return copy(gb.at[0, k, p, x], gb.at[1, k, q, x], ts.at[k], tr.at[k], at_flip)
+        slot = t_slots[k // 2]
+        return copy(gb.at[0, k, p, x], gb.at[1, k, slot, x], ts.at[k], tr.at[k], (z, p, slot, x))
 
     def t_send(k):
-        pl.when(p != q)(lambda: t_copy(k).start())
-        sends.append(lambda: pl.when(p != q)(lambda: t_copy(k).wait_send()))
+        pl.when(delta != 0)(lambda: t_copy(k).start())
+        sends.append(lambda: pl.when(delta != 0)(lambda: t_copy(k).wait_send()))
 
     def t_wait(k):
-        pl.when(p != q)(lambda: copy(
-            gb.at[1, k, p, x], gb.at[1, k, p, x], ts.at[k], tr.at[k], at_flip).wait_recv())
+        ref = gb.at[1, k, p, x]
+        guarded(1, k, p, lambda: copy(ref, ref, ts.at[k], tr.at[k], at_core).wait_recv())
 
     def c_copy(j, block_q, ri, device):
         if ri < 2:
@@ -172,11 +187,13 @@
         c_send(j, q, 0, at_qr)
         c_send(j, q, 1, at_ql)
 
-    def c_forward(j):
-        c_copy(j, ql, 0, at_qr).wait_recv()
-        c_send(j, ql, 2, at_qr)
-        c_copy(j, qr, 1, at_qr).wait_recv()
-        c_send(j, qr, 3, at_ql)
+    def c_fwd(way, j):
+        if way == 0:
+            c_copy(j, ql, 0, at_qr).wait_recv()
+            c_send(j, ql, 2, at_qr)
+        else:
+            c_copy(j, qr, 1, at_qr).wait_recv()
+            c_send(j, qr, 3, at_ql)
 
     def c_last(j):
         c_copy(j, qo, 2, at_qr).wait_recv()
@@ -191,12 +208,14 @@
             wy_copy(q, ri, device).start()
             sends.append(lambda ri=ri, device=device: wy_copy(q, ri, device).wait_send())
 
-    def wy_forward():
-        wy_copy(ql, 0, at_qr).wait_recv()
-        pl.when(core == 0)(lambda: wy_copy(ql, 2, at_qr).start())
-        wy_copy(qr, 1, at_qr).wait_recv()
-        pl.when(core == 1)(lambda: wy_copy(qr, 2, at_ql).start())
-        sends.append(lambda: wy_copy(ql, 2, at_qr).wait_send())
+    def wy_fwd(way):
+        if way == 0:
+            wy_copy(ql, 0, at_qr).wait_recv()
+            pl.when(core == 0)(lambda: wy_copy(ql, 2, at_qr).start())
+        else:
+            wy_copy(qr, 1, at_qr).wait_recv()
+            pl.when(core == 1)(lambda: wy_copy(qr, 2, at_ql).start())
+            sends.append(lambda: wy_copy(ql, 2, at_qr).wait_send())
 
     def wz_copy(m, block_q, slice_z, ri, device):
         ref = ws.at[block_q, slice_z]
@@ -219,7 +238,18 @@
         if step <= 3:
             wz_copy(m, block_q, (z + step * up + 8) % 8, 3 + step, at_core).wait_recv()
 
+    def wz_step(m, step):
+        if step > 1:
+            wz_wait(m, step - 1)
+        elif m == 2:
+            wy_copy(qo, 2, at_qr).wait_recv()
+        wz_send(m, step)
+
     def kg_part(j):
+        if j == 0:
+            for k in range(4):
+                g_core_wait(0, k)
+        c_last(j)
         turn = one_hot(128, 128, lambda r, c: c == 4 * (r % 32) + r // 32)
         for b in range(4):
             cpt[:, b * 512:(b + 1) * 512] = dot_nt(turn, cb[b, j]).astype(BF)
@@ -235,27 +265,34 @@
             for s in range(4):
                 rs_out[j, s, :, cols] = first[8 * s:8 * s + 8]
                 rs_out[j, 4 + s, :, cols] = second[8 * s:8 * s + 8]
-
-    def rs_copy(j, step):
-        return copy(rs_out.at[j, (z + step) % 8], rs_in.at[j, step - 1],
-                    rss.at[j, step - 1], rsr.at[j, step - 1], at_z(step))
-
-    def rs_send(j):
-        for step in (4, 3, 5, 2, 6, 1, 7):
-            rs_copy(j, step).start()
-            sends.append(lambda step=step: rs_copy(j, step).wait_send())
+        rs_send(j, 1)
+
+    def rs_copy(j, step, way):
+        if way == 0:
+            ref, slot, device = rs_out.at[j, (z + (5 - step) * up + 8) % 8], step - 1, at_z(up)
+        else:
+            ref, slot, device = rs_out.at[j, (z - (4 - step) * up + 8) % 8], 3 + step, at_z(-up)
+        return copy(ref, rs_in.at[j, slot], rss.at[j, slot], rsr.at[j, slot], device)
+
+    def rs_send(j, step):
+        for way in range(2 if step < 4 else 1):
+            rs_copy(j, step, way).start()
+            sends.append(lambda way=way: rs_copy(j, step, way).wait_send())
+
+    def rs_step(j, step):
+        rs_copy(j, step, 0).wait_recv()
+        rs_out[j, (z + (4 - step) * up + 8) % 8] += rs_in[j, step - 1]
+        rs_copy(j, step, 1).wait_recv()
+        rs_out[j, (z - (3 - step) * up + 8) % 8] += rs_in[j, 3 + step]
+        rs_send(j, step + 1)
 
     def ag_copy(j, step, slice_z):
         ref = ag.at[j, slice_z]
         return copy(ref, ref, ags.at[j, step - 1], agr.at[j, step - 1], at_z(step))
 
     def rs_finish(j):
-        for step in range(1, 8):
-            rs_copy(j, step).wait_recv()
-        total = rs_out[j, z]
-        for step in range(7):
-            total = total + rs_in[j, step]
-        total = total * (16384.0 ** -0.5)
+        rs_copy(j, 4, 0).wait_recv()
+        total = (rs_out[j, z] + rs_in[j, 3]) * (16384.0 ** -0.5)
         ag[j, z] = jnp.concatenate([total[:, :768], total[:, 768:]], 0).astype(BF)
         for step in (4, 3, 5, 2, 6, 1, 7):
             ag_copy(j, step, z).start()
@@ -266,6 +303,8 @@
             ag_copy(j, step, (z - step + 8) % 8).wait_recv()
 
     def kg_store():
+        for j in range(3):
+            ag_wait(j)
         rows = ag[...].reshape(384, 768)
         for h in range(2):
             def hit(r, c, h=h):
@@ -295,98 +334,130 @@
         acc[...] = total
 
     def cg_add(k):
-        for b in (ql, qr, qo):
-            acc[...] += dot_nt(gb[1, k, b].reshape(512, 384), weights(b, k))
+        if k == 0:
+            for m in range(3):
+                wz_wait(m, 4)
+        g_core_wait(1, k)
+        for slot, b in ((0, ql), (3, qr), (1 if k < 2 else 2, qo)):
+            acc[...] += dot_nt(gb[1, k, slot].reshape(512, 384), weights(b, k))
 
     def cg_store():
         back = one_hot(384, 384, lambda r, c: c == 4 * (r % 96) + r // 96)
         cg_ref[...] = dot_nn(acc[...].astype(BF), back).astype(BF)
 
-    for k in range(4):
-        g_twin_send(0, k)
-        g_own(0, k)
+    g_twin_send(0, 0)
+    g_own(0, 0)
+    g_twin_send(0, 1)
+    g_own(0, 1)
+    g_twin_send(0, 2)
+    g_twin_send(0, 3)
     wy_own()
+    g_own(0, 2)
+    g_fwd_own(0, 0)
+    g_own(0, 3)
+    g_fwd_own(0, 1)
     c_own(0)
     g_twin(0, 0)
-    wy_forward()
-    wz_send(0, 1)
-    wz_send(1, 1)
-    g_forward(0, 0)
+    g_fwd_own(0, 2)
+    g_twin(0, 1)
+    g_core_own(0, 0)
+    g_fwd_own(0, 3)
+    g_core_own(0, 1)
+    g_twin(0, 2)
+    g_twin(0, 3)
+    wy_fwd(0)
+    wy_fwd(1)
+    wz_step(0, 1)
+    wz_step(1, 1)
     c_own(1)
-    g_twin(0, 1)
-    wy_copy(qo, 2, at_qr).wait_recv()
-    wz_send(2, 1)
-    c_forward(0)
-    g_forward(0, 1)
-    g_last(0, 0)
+    g_fwd_twin(0, 0)
+    c_fwd(0, 0)
+    c_fwd(1, 0)
+    g_fwd_twin(0, 1)
+    wz_step(0, 2)
+    wz_step(1, 2)
+    g_fwd_twin(0, 2)
+    g_fwd_twin(0, 3)
     c_own(2)
-    g_twin(0, 2)
-    for m in range(3):
-        wz_wait(m, 1)
-        wz_send(m, 2)
-    g_forward(0, 2)
-    g_last(0, 1)
-    for k in range(4):
-        t_send(k)
-    g_twin(0, 3)
-    c_last(0)
-    c_forward(1)
-    for m in range(3):
-        wz_wait(m, 2)
-        wz_send(m, 3)
-    g_forward(0, 3)
-    g_last(0, 2)
-    c_forward(2)
-    g_last(0, 3)
-    for m in range(3):
-        wz_wait(m, 3)
-        wz_send(m, 4)
-    for k in range(4):
-        g_core_wait(0, k)
-    c_last(1)
-    for k in range(4):
-        t_wait(k)
-        g_twin_send(1, k)
-        g_own(1, k)
+    g_core_twin(0, 0)
+    g_core_own(0, 2)
+    g_core_own(0, 3)
+    wz_step(2, 1)
+    g_core_twin(0, 1)
+    wz_step(0, 3)
+    wz_step(1, 3)
+    g_core_twin(0, 2)
+    g_core_twin(0, 3)
+    c_fwd(0, 1)
+    c_fwd(1, 1)
+    t_send(0)
+    t_send(2)
+    wz_step(2, 2)
     kg_part(0)
-    rs_send(0)
+    cg_own()
+    c_fwd(0, 2)
+    c_fwd(1, 2)
+    t_send(1)
+    wz_step(0, 4)
+    wz_step(1, 4)
+    kg_part(1)
+    rs_step(0, 1)
+    wz_step(2, 3)
+    t_wait(0)
+    g_twin_send(1, 0)
+    g_own(1, 0)
+    t_wait(2)
+    g_twin_send(1, 2)
+    g_own(1, 2)
+    kg_part(2)
+    t_wait(1)
+    g_twin_send(1, 1)
+    g_own(1, 1)
+    t_send(3)
+    rs_step(1, 1)
+    rs_step(0, 2)
+    wz_step(2, 4)
+    g_fwd_own(1, 0)
+    rs_step(2, 1)
     g_twin(1, 0)
-    g_forward(1, 0)
-    kg_part(1)
-    rs_send(1)
+    g_fwd_own(1, 2)
+    g_twin(1, 2)
+    g_fwd_own(1, 1)
+    rs_step(1, 2)
+    rs_step(0, 3)
     g_twin(1, 1)
-    g_forward(1, 1)
-    g_last(1, 0)
-    c_last(2)
-    kg_part(2)
-    rs_send(2)
-    g_twin(1, 2)
-    g_forward(1, 2)
-    g_last(1, 1)
+    t_wait(3)
+    g_twin_send(1, 3)
+    g_own(1, 3)
+    rs_step(2, 2)
+    g_fwd_twin(1, 0)
+    rs_step(1, 3)
     rs_finish(0)
-    cg_own()
+    g_core_own(1, 0)
+    g_fwd_twin(1, 2)
+    rs_step(2, 3)
     g_twin(1, 3)
-    g_forward(1, 3)
-    g_last(1, 2)
-    for m in range(3):
-        wz_wait(m, 4)
+    g_fwd_twin(1, 1)
     rs_finish(1)
-    g_core_wait(1, 0)
+    g_core_own(1, 2)
+    g_core_twin(1, 0)
+    g_core_own(1, 1)
+    g_fwd_own(1, 3)
+    g_core_twin(1, 2)
     cg_add(0)
-    g_last(1, 3)
-    g_core_wait(1, 1)
+    g_fwd_twin(1, 3)
+    g_core_twin(1, 1)
+    rs_finish(2)
+    cg_add(2)
     cg_add(1)
-    rs_finish(2)
-    g_core_wait(1, 2)
-    cg_add(2)
-    g_core_wait(1, 3)
+    g_core_own(1, 3)
+    g_core_twin(1, 3)
     cg_add(3)
+    kg_store()
     cg_store()
-    for j in range(3):
-        ag_wait(j)
-    kg_store()
     for wait in sends:
         wait()
+
 
 def local(context, out_grad, kept_values, keep_codes):
     dma = pltpu.SemaphoreType.DMA

time: 117 us -> 101 us (0.86)
  the two profiles are of different devices: /device:TPU:21 before, /device:TPU:1 now
where the time goes in v2:
time: 101 us; the launch traced here: 100 us
  Pallas kernels  96.8 us (96%)
  local copies, waits for them, and re-layouts  2.66 us (3%)
    pallas_call x1, Pallas kernels, local(): pl.pallas_call(kernel, out_shape=(jax.ShapeDtypeStruct((512, 384), BF), j...  96.8 us
    unnamed x4, local copies, waits for them, and re-layouts  2.66 us

profile of v2, /device:TPU:1, one launch (start us, length us, event | category | flops | bytes accessed | tf_op | source)
XLA Modules:
  0.0 100.1 jit_solution(13019361193934775605)
XLA Ops:
  0.6 96.8 %sparse_backward.1 = (bf16[512,384]{1,0:T(8,128)(2,1)}, bf16[192,1536]{1,0:T(8,128)(2,1)}) custom-call(bf16[512,384]{1,0:T(8,128)(2,1)} %ctx_hbm.1, bf16[128,1536]{1,0:T(8,128)(2,1)} %grad_hbm.1, bf16[192,1536]{1,0:T(8,128)(2,1)} %kept_hbm.1, s32[96,1536]{1,0:T(8,128)} %codes_hbm.1), custom_call_target="tpu_custom_call" | custom-call | flops 4831838208 | bytes 3145728 | tf_op jit(solution)/shard_map/sparse_backward/pallas_call | solution.py:464
  97.5 0.0 copy-start
  97.5 1.8 %copy.8 = bf16[512,384]{1,0:T(8,128)(2,1)} copy(bf16[512,384]{1,0:T(8,128)(2,1)} %get-tuple-element.4) | data formatting | bytes 786432
  99.3 0.0 copy-done
  99.3 0.8 copy.9
Async XLA Ops:
  97.5 1.9 %copy-start = (bf16[192,1536]{1,0:T(8,128)(2,1)S(1)}, bf16[192,1536]{1,0:T(8,128)(2,1)}, u32[]{:S(2)}) copy-start(bf16[192,1536]{1,0:T(8,128)(2,1)} %get-tuple-element.5) | copy-start | bytes 1769476

commit v3 on v2

--- a/solution.py
+++ b/solution.py
@@ -22,7 +22,7 @@
 
 def kernel(
     ctx_hbm, grad_hbm, kept_hbm, codes_hbm, cg_ref, kg_ref,
-    gb, cb, cpt, ws, kept_v, codes_v, rs_out, rs_in, ag, acc,
+    gb, cb, cpt, ws, kept_v, codes_v, rs_out, rs_in, ag, acc, wd,
     load_sem, gs, gr, ts, tr, cs, cr, wys, wyr, wzs, wzr, rss, rsr, ags, agr,
 ):
     z = lax.axis_index("rep")
@@ -86,28 +86,31 @@
         pl.semaphore_signal(
             barrier, inc=1, device_id=(z, p, t_slots[1], x), device_id_type=MESH)
 
-    for ld in loads:
+    for ld in loads[:4]:
         ld.wait()
-    split = one_hot(192, 192, lambda r, c: c == 2 * (r % 96) + r // 96)
-    for k in range(4):
-        cols = pl.ds(k * 384, 384)
-        both = dot_nn(split, kept_v[:, cols]).astype(BF)
-        numbers = codes_v[:, cols].astype(F32).astype(BF)
-        ws[q, k] = both[:144]
-        ws[q, 4 + k, 0:48] = both[144:]
-        ws[q, 4 + k, 48:144] = numbers
-
     pl.semaphore_wait(barrier, jnp.where(delta == 0, 14, jnp.where(delta == 2, 16, 15)))
+
+    def prep():
+        loads[7].wait()
+        loads[8].wait()
+        split = one_hot(192, 192, lambda r, c: c == 2 * (r % 96) + r // 96)
+        for k in range(4):
+            cols = pl.ds(k * 384, 384)
+            both = dot_nn(split, kept_v[:, cols]).astype(BF)
+            numbers = codes_v[:, cols].astype(F32).astype(BF)
+            ws[q, k] = both[:144]
+            ws[q, 4 + k, 0:48] = both[144:]
+            ws[q, 4 + k, 48:144] = numbers
 
     def guarded(ph, k, block_p, run):
         if ph == 0:
             run()
         else:
-            pl.when(block_p != (2 if k < 2 else 1))(run)
+            pl.when(block_p != (2 if k < 4 else 1))(run)
 
     def g_copy(ph, k, block, si, ri, device):
-        ref = gb.at[ph, k, block[0], block[1]]
-        return copy(ref, ref, gs.at[ph * 4 + k, si], gr.at[ph * 4 + k, ri], device)
+        ref = gb.at[ph, k // 2, block[0], block[1], pl.ds(k % 2 * 64, 64)]
+        return copy(ref, ref, gs.at[ph * 8 + k, si], gr.at[ph * 8 + k, ri], device)
 
     def g_send(ph, k, block, si, ri, device):
         guarded(ph, k, block[0], lambda: g_copy(ph, k, block, si, ri, device).start())
@@ -118,8 +121,8 @@
         guarded(ph, k, block[0], lambda: g_copy(ph, k, block, 0, ri, at_core).wait_recv())
 
     def g_row(ph, k, block_p, si, ri):
-        ref = gb.at[ph, k, block_p]
-        return copy(ref, ref, gs.at[ph * 4 + k, si], gr.at[ph * 4 + k, ri], at_core)
+        ref = gb.at[ph, k // 2, block_p, pl.ds(0, 4), pl.ds(k % 2 * 64, 64)]
+        return copy(ref, ref, gs.at[ph * 8 + k, si], gr.at[ph * 8 + k, ri], at_core)
 
     def g_core(ph, k, block_p, si, ri):
         guarded(ph, k, block_p, lambda: g_row(ph, k, block_p, si, ri).start())
@@ -161,22 +164,20 @@
         g_core(ph, k, twin_p, 8, 8)
 
     def t_copy(k):
-        slot = t_slots[k // 2]
-        return copy(gb.at[0, k, p, x], gb.at[1, k, slot, x], ts.at[k], tr.at[k], (z, p, slot, x))
+        slot, rows = t_slots[k // 4], pl.ds(k % 2 * 64, 64)
+        return copy(gb.at[0, k // 2, p, x, rows], gb.at[1, k // 2, slot, x, rows],
+                    ts.at[k], tr.at[k], (z, p, slot, x))
 
     def t_send(k):
         pl.when(delta != 0)(lambda: t_copy(k).start())
         sends.append(lambda: pl.when(delta != 0)(lambda: t_copy(k).wait_send()))
 
     def t_wait(k):
-        ref = gb.at[1, k, p, x]
+        ref = gb.at[1, k // 2, p, x, pl.ds(k % 2 * 64, 64)]
         guarded(1, k, p, lambda: copy(ref, ref, ts.at[k], tr.at[k], at_core).wait_recv())
 
     def c_copy(j, block_q, ri, device):
-        if ri < 2:
-            ref = cb.at[block_q, j]
-        else:
-            ref = cb.at[block_q, j, pl.ds((ri - 2) * 256, 256)]
+        ref = cb.at[block_q, j, pl.ds((0, 256, 0, 256, 256, 0)[ri], 256)]
         return copy(ref, ref, cs.at[j, ri], cr.at[j, ri], device)
 
     def c_send(j, block_q, ri, device):
@@ -184,8 +185,11 @@
         sends.append(lambda: c_copy(j, block_q, ri, device).wait_send())
 
     def c_own(j):
+        loads[4 + j].wait()
         c_send(j, q, 0, at_qr)
         c_send(j, q, 1, at_ql)
+        c_send(j, q, 4, at_qr)
+        c_send(j, q, 5, at_ql)
 
     def c_fwd(way, j):
         if way == 0:
@@ -196,8 +200,8 @@
             c_send(j, qr, 3, at_ql)
 
     def c_last(j):
-        c_copy(j, qo, 2, at_qr).wait_recv()
-        c_copy(j, qo, 3, at_qr).wait_recv()
+        for ri, block_q in ((4, ql), (5, qr), (2, qo), (3, qo)):
+            c_copy(j, block_q, ri, at_qr).wait_recv()
 
     def wy_copy(block_q, ri, device):
         ref = ws.at[block_q, z]
@@ -246,9 +250,6 @@
         wz_send(m, step)
 
     def kg_part(j):
-        if j == 0:
-            for k in range(4):
-                g_core_wait(0, k)
         c_last(j)
         turn = one_hot(128, 128, lambda r, c: c == 4 * (r % 32) + r // 32)
         for b in range(4):
@@ -328,131 +329,214 @@
         return jnp.concatenate([w0, w1, w2, w3], 0).astype(BF)
 
     def cg_own():
+        for k in range(8):
+            g_core_wait(0, k)
         total = jnp.zeros((512, 384), F32)
         for k in range(4):
             total = total + dot_nt(gb[0, k, q].reshape(512, 384), weights(q, k))
-        acc[...] = total
-
-    def cg_add(k):
+        acc[...] = total.reshape(4, 128, 384)
+
+    def widen(k):
         if k == 0:
             for m in range(3):
                 wz_wait(m, 4)
+        for m, block_q in enumerate((ql, qr, qo)):
+            wd[m, k] = weights(block_q, k)
+
+    def cg_add(k):
         g_core_wait(1, k)
-        for slot, b in ((0, ql), (3, qr), (1 if k < 2 else 2, qo)):
-            acc[...] += dot_nt(gb[1, k, slot].reshape(512, 384), weights(b, k))
+        rows = slice(k % 2 * 64, k % 2 * 64 + 64)
+        total = acc[:, rows]
+        for m, slot in enumerate((0, 3, 1 if k < 4 else 2)):
+            part = gb[1, k // 2, slot, :, rows].reshape(256, 384)
+            total = total + dot_nt(part, wd[m, k // 2]).reshape(4, 64, 384)
+        acc[:, rows] = total
 
     def cg_store():
         back = one_hot(384, 384, lambda r, c: c == 4 * (r % 96) + r // 96)
-        cg_ref[...] = dot_nn(acc[...].astype(BF), back).astype(BF)
+        cg_ref[...] = dot_nn(acc[...].reshape(512, 384).astype(BF), back).astype(BF)
 
     g_twin_send(0, 0)
     g_own(0, 0)
     g_twin_send(0, 1)
     g_own(0, 1)
     g_twin_send(0, 2)
+    g_own(0, 2)
     g_twin_send(0, 3)
+    g_own(0, 3)
+    g_twin_send(0, 4)
+    g_twin_send(0, 5)
+    g_twin_send(0, 7)
+    prep()
     wy_own()
-    g_own(0, 2)
     g_fwd_own(0, 0)
-    g_own(0, 3)
+    g_own(0, 4)
+    g_twin(0, 0)
     g_fwd_own(0, 1)
+    g_own(0, 5)
+    g_twin(0, 1)
+    g_fwd_own(0, 2)
+    g_own(0, 6)
+    g_twin(0, 2)
+    g_twin_send(0, 6)
+    g_fwd_own(0, 3)
+    g_own(0, 7)
+    g_twin(0, 3)
     c_own(0)
-    g_twin(0, 0)
-    g_fwd_own(0, 2)
-    g_twin(0, 1)
     g_core_own(0, 0)
-    g_fwd_own(0, 3)
+    g_twin(0, 4)
+    g_fwd_own(0, 4)
+    g_fwd_twin(0, 0)
+    g_twin(0, 5)
+    g_twin(0, 7)
     g_core_own(0, 1)
-    g_twin(0, 2)
-    g_twin(0, 3)
+    g_fwd_twin(0, 1)
+    g_fwd_own(0, 5)
+    g_fwd_twin(0, 2)
+    g_core_own(0, 2)
+    g_fwd_own(0, 6)
     wy_fwd(0)
+    wz_step(0, 1)
     wy_fwd(1)
-    wz_step(0, 1)
     wz_step(1, 1)
+    g_fwd_twin(0, 3)
+    g_fwd_twin(0, 4)
+    g_twin(0, 6)
     c_own(1)
-    g_fwd_twin(0, 0)
+    g_core_own(0, 3)
+    g_core_twin(0, 0)
+    g_fwd_own(0, 7)
+    g_fwd_twin(0, 5)
+    c_own(2)
     c_fwd(0, 0)
     c_fwd(1, 0)
-    g_fwd_twin(0, 1)
+    g_fwd_twin(0, 7)
     wz_step(0, 2)
+    g_core_twin(0, 1)
+    g_core_own(0, 4)
+    g_core_twin(0, 2)
     wz_step(1, 2)
-    g_fwd_twin(0, 2)
-    g_fwd_twin(0, 3)
-    c_own(2)
-    g_core_twin(0, 0)
-    g_core_own(0, 2)
-    g_core_own(0, 3)
+    g_core_twin(0, 3)
+    g_core_twin(0, 4)
     wz_step(2, 1)
-    g_core_twin(0, 1)
+    g_core_own(0, 5)
     wz_step(0, 3)
+    g_fwd_twin(0, 6)
+    g_core_own(0, 6)
+    g_core_twin(0, 5)
+    g_core_twin(0, 7)
+    c_fwd(0, 1)
     wz_step(1, 3)
-    g_core_twin(0, 2)
-    g_core_twin(0, 3)
-    c_fwd(0, 1)
     c_fwd(1, 1)
+    t_send(1)
+    g_core_own(0, 7)
+    g_core_twin(0, 6)
+    wz_step(2, 2)
+    cg_own()
+    wz_step(0, 4)
+    c_fwd(0, 2)
+    c_fwd(1, 2)
     t_send(0)
     t_send(2)
-    wz_step(2, 2)
+    t_send(3)
+    t_send(5)
+    t_send(6)
+    wz_step(1, 4)
+    t_send(4)
+    t_send(7)
+    wz_step(2, 3)
     kg_part(0)
-    cg_own()
-    c_fwd(0, 2)
-    c_fwd(1, 2)
-    t_send(1)
-    wz_step(0, 4)
-    wz_step(1, 4)
     kg_part(1)
+    wz_step(2, 4)
+    t_wait(1)
+    g_twin_send(1, 1)
+    g_own(1, 1)
     rs_step(0, 1)
-    wz_step(2, 3)
+    kg_part(2)
     t_wait(0)
     g_twin_send(1, 0)
     g_own(1, 0)
+    rs_step(1, 1)
     t_wait(2)
     g_twin_send(1, 2)
     g_own(1, 2)
-    kg_part(2)
-    t_wait(1)
-    g_twin_send(1, 1)
-    g_own(1, 1)
-    t_send(3)
-    rs_step(1, 1)
-    rs_step(0, 2)
-    wz_step(2, 4)
-    g_fwd_own(1, 0)
-    rs_step(2, 1)
-    g_twin(1, 0)
-    g_fwd_own(1, 2)
-    g_twin(1, 2)
     g_fwd_own(1, 1)
-    rs_step(1, 2)
-    rs_step(0, 3)
-    g_twin(1, 1)
+    widen(0)
     t_wait(3)
     g_twin_send(1, 3)
     g_own(1, 3)
+    rs_step(0, 2)
+    t_wait(5)
+    g_twin_send(1, 5)
+    g_own(1, 5)
+    t_wait(6)
+    g_twin_send(1, 6)
+    g_own(1, 6)
+    widen(1)
+    rs_step(2, 1)
+    t_wait(4)
+    g_twin_send(1, 4)
+    g_own(1, 4)
+    t_wait(7)
+    g_twin_send(1, 7)
+    rs_step(1, 2)
+    g_own(1, 7)
+    g_fwd_own(1, 0)
+    g_twin(1, 1)
+    g_core_own(1, 1)
+    g_fwd_own(1, 2)
+    widen(2)
+    rs_step(0, 3)
+    g_twin(1, 0)
+    g_twin(1, 2)
+    g_fwd_own(1, 3)
+    g_fwd_own(1, 5)
+    widen(3)
     rs_step(2, 2)
+    g_twin(1, 3)
+    g_fwd_own(1, 4)
+    rs_step(1, 3)
+    g_twin(1, 5)
+    g_fwd_own(1, 6)
+    g_twin(1, 6)
+    g_fwd_own(1, 7)
+    rs_finish(0)
+    g_fwd_twin(1, 1)
+    g_core_own(1, 0)
+    g_twin(1, 4)
     g_fwd_twin(1, 0)
-    rs_step(1, 3)
-    rs_finish(0)
-    g_core_own(1, 0)
+    g_twin(1, 7)
     g_fwd_twin(1, 2)
     rs_step(2, 3)
-    g_twin(1, 3)
-    g_fwd_twin(1, 1)
+    g_core_own(1, 2)
+    g_fwd_twin(1, 3)
     rs_finish(1)
-    g_core_own(1, 2)
+    g_fwd_twin(1, 5)
+    g_fwd_twin(1, 6)
+    g_core_own(1, 3)
+    g_core_twin(1, 1)
+    g_core_own(1, 5)
+    g_fwd_twin(1, 4)
     g_core_twin(1, 0)
-    g_core_own(1, 1)
-    g_fwd_own(1, 3)
+    cg_add(1)
+    g_core_own(1, 4)
+    g_fwd_twin(1, 7)
+    rs_finish(2)
     g_core_twin(1, 2)
     cg_add(0)
-    g_fwd_twin(1, 3)
-    g_core_twin(1, 1)
-    rs_finish(2)
+    g_core_own(1, 6)
+    g_core_twin(1, 3)
+    g_core_twin(1, 5)
     cg_add(2)
-    cg_add(1)
-    g_core_own(1, 3)
-    g_core_twin(1, 3)
+    g_core_own(1, 7)
+    g_core_twin(1, 6)
     cg_add(3)
+    g_core_twin(1, 4)
+    cg_add(5)
+    g_core_twin(1, 7)
+    cg_add(6)
+    cg_add(4)
+    cg_add(7)
     kg_store()
     cg_store()
     for wait in sends:
@@ -479,15 +563,16 @@
             pltpu.VMEM((3, 8, 8, 1536), F32),
             pltpu.VMEM((3, 7, 8, 1536), F32),
             pltpu.VMEM((3, 8, 16, 768), BF),
-            pltpu.VMEM((512, 384), F32),
+            pltpu.VMEM((4, 128, 384), F32),
+            pltpu.VMEM((3, 4, 384, 384), BF),
             dma((9,)),
 
-            dma((8, 9)),
-            dma((8, 9)),
-            dma((4,)),
-            dma((4,)),
-            dma((3, 4)),
-            dma((3, 4)),
+            dma((16, 9)),
+            dma((16, 9)),
+            dma((8,)),
+            dma((8,)),
+            dma((3, 6)),
+            dma((3, 6)),
             dma((3,)),
             dma((3,)),
             dma((3, 7)),

time: 101 us -> 100 us (0.990)
  no operation moved by 1% of the time
where the time goes in v3:
time: 100 us; the launch traced here: 99.7 us
  Pallas kernels  96.4 us (96%)
  local copies, waits for them, and re-layouts  2.66 us (3%)
    pallas_call x1, Pallas kernels, local(): pl.pallas_call(kernel, out_shape=(jax.ShapeDtypeStruct((512, 384), BF), j...  96.4 us
    unnamed x4, local copies, waits for them, and re-layouts  2.66 us

profile of v3, /device:TPU:1, one launch (start us, length us, event | category | flops | bytes accessed | tf_op | source)
XLA Modules:
  0.0 99.7 jit_solution(1402043202633177526)
XLA Ops:
  0.6 96.4 %sparse_backward.1 = (bf16[512,384]{1,0:T(8,128)(2,1)}, bf16[192,1536]{1,0:T(8,128)(2,1)}) custom-call(bf16[512,384]{1,0:T(8,128)(2,1)} %ctx_hbm.1, bf16[128,1536]{1,0:T(8,128)(2,1)} %grad_hbm.1, bf16[192,1536]{1,0:T(8,128)(2,1)} %kept_hbm.1, s32[96,1536]{1,0:T(8,128)} %codes_hbm.1), custom_call_target="tpu_custom_call" | custom-call | flops 4831838208 | bytes 3145728 | tf_op jit(solution)/shard_map/sparse_backward/pallas_call | solution.py:548
  97.0 0.0 copy-start
  97.0 1.8 %copy.8 = bf16[512,384]{1,0:T(8,128)(2,1)} copy(bf16[512,384]{1,0:T(8,128)(2,1)} %get-tuple-element.4) | data formatting | bytes 786432
  98.9 0.0 copy-done
  98.9 0.8 copy.9
Async XLA Ops:
  97.0 1.9 %copy-start = (bf16[192,1536]{1,0:T(8,128)(2,1)S(1)}, bf16[192,1536]{1,0:T(8,128)(2,1)}, u32[]{:S(2)}) copy-start(bf16[192,1536]{1,0:T(8,128)(2,1)} %get-tuple-element.5) | copy-start | bytes 1769476

commit v4 on v3

--- a/solution.py
+++ b/solution.py
@@ -21,7 +21,7 @@
     return jnp.where(hit(r, c), 1.0, 0.0).astype(BF)
 
 def kernel(
-    ctx_hbm, grad_hbm, kept_hbm, codes_hbm, cg_ref, kg_ref,
+    ctx_hbm, grad_hbm, kept_hbm, codes_hbm, cg_hbm, kg_hbm, cg_ref, kg_ref,
     gb, cb, cpt, ws, kept_v, codes_v, rs_out, rs_in, ag, acc, wd,
     load_sem, gs, gr, ts, tr, cs, cr, wys, wyr, wzs, wzr, rss, rsr, ags, agr,
 ):
@@ -302,6 +302,9 @@
     def ag_wait(j):
         for step in range(1, 8):
             ag_copy(j, step, (z - step + 8) % 8).wait_recv()
+
+    kg_out = pltpu.make_async_copy(kg_ref, kg_hbm, load_sem.at[9])
+    cg_out = pltpu.make_async_copy(cg_ref, cg_hbm, load_sem.at[10])
 
     def kg_store():
         for j in range(3):
@@ -536,11 +539,15 @@
     g_core_twin(1, 7)
     cg_add(6)
     cg_add(4)
-    cg_add(7)
     kg_store()
-    cg_store()
+    kg_out.start()
     for wait in sends:
         wait()
+    cg_add(7)
+    cg_store()
+    cg_out.start()
+    kg_out.wait()
+    cg_out.wait()
 
 
 def local(context, out_grad, kept_values, keep_codes):
@@ -552,8 +559,10 @@
             jax.ShapeDtypeStruct((192, 1536), BF),
         ),
         in_specs=[pl.BlockSpec(memory_space=pl.ANY)] * 4,
-        out_specs=(pl.BlockSpec(memory_space=pltpu.VMEM),) * 2,
+        out_specs=(pl.BlockSpec(memory_space=pl.ANY),) * 2,
         scratch_shapes=[
+            pltpu.VMEM((512, 384), BF),
+            pltpu.VMEM((192, 1536), BF),
             pltpu.VMEM((2, 4, 4, 4, 128, 384), BF),
             pltpu.VMEM((4, 3, 512, 128), BF),
             pltpu.VMEM((128, 2048), BF),
@@ -565,7 +574,7 @@
             pltpu.VMEM((3, 8, 16, 768), BF),
             pltpu.VMEM((4, 128, 384), F32),
             pltpu.VMEM((3, 4, 384, 384), BF),
-            dma((9,)),
+            dma((11,)),
 
             dma((16, 9)),
             dma((16, 9)),

time: 100 us -> 101 us (1.010)
  no operation moved by 1% of the time
where the time goes in v4:
time: 101 us; the launch traced here: 100 us
  Pallas kernels  97.1 us (96%)
  local copies, waits for them, and re-layouts  2.66 us (3%)
    pallas_call x1, Pallas kernels, local(): pl.pallas_call(kernel, out_shape=(jax.ShapeDtypeStruct((512, 384), BF), j...  97.1 us
    unnamed x4, local copies, waits for them, and re-layouts  2.66 us

profile of v4, /device:TPU:1, one launch (start us, length us, event | category | flops | bytes accessed | tf_op | source)
XLA Modules:
  0.0 100.4 jit_solution(11173086885660012931)
XLA Ops:
  0.6 97.1 %sparse_backward.1 = (bf16[512,384]{1,0:T(8,128)(2,1)}, bf16[192,1536]{1,0:T(8,128)(2,1)}) custom-call(bf16[512,384]{1,0:T(8,128)(2,1)} %ctx_hbm.1, bf16[128,1536]{1,0:T(8,128)(2,1)} %grad_hbm.1, bf16[192,1536]{1,0:T(8,128)(2,1)} %kept_hbm.1, s32[96,1536]{1,0:T(8,128)} %codes_hbm.1), custom_call_target="tpu_custom_call" | custom-call | flops 4831838208 | bytes 3145728 | tf_op jit(solution)/shard_map/sparse_backward/pallas_call | solution.py:555
  97.7 0.0 copy-start
  97.7 1.8 %copy.8 = bf16[512,384]{1,0:T(8,128)(2,1)} copy(bf16[512,384]{1,0:T(8,128)(2,1)} %get-tuple-element.4) | data formatting | bytes 786432
  99.5 0.0 copy-done
  99.5 0.8 copy.9
Async XLA Ops:
  97.7 1.9 %copy-start = (bf16[192,1536]{1,0:T(8,128)(2,1)S(1)}, bf16[192,1536]{1,0:T(8,128)(2,1)}, u32[]{:S(2)}) copy-start(bf16[192,1536]{1,0:T(8,128)(2,1)} %get-tuple-element.5) | copy-start | bytes 1769476
